TPU v7x, 768 devices: a whole 4x8x12 slice. The times are simulated.
768 devices in a mesh: outer: 96 (over z, x, core), node: 8 (over y).
Axes of the slice: x: 4, y: 8, z: 12, core: 2. Of those that a mesh axis runs over, the one named last changes fastest.
Arguments:
- bag_grads: float32 [24576, 128], P(('outer', 'node')), may hold values from -6 to 6
- bag_lengths: int32 [768, 32], P(('outer', 'node')), may hold values from 1 to 32, 512 in all within a row
- look_slot: int32 [768, 512], P(('outer', 'node')), may hold values from 0 to 191, as said below
- group_slot: int32 [768, 8, 24], P(('outer', 'node')), may hold values from 0 to 191, as said below
- owner_row: int32 [768, 96, 2], P(('outer', 'node')), may hold values from 0 to 1023, as said below
- table: float32 [786432, 128], P(('outer', 'node')), may hold values from -3 to 3
- accum: float32 [786432], P(('outer', 'node')), may hold values from 0.5 to 4
Outputs:
- new_table: float32 [786432, 128], P(('outer', 'node'))
- new_accum: float32 [786432], P(('outer', 'node'))
- fresh_rows: bfloat16 [393216, 128], P(('outer', 'node'))
Inputs may be any that keep to these rules, and one draw needn't show every extreme that they name: `look_slot`: entry m * 24 + c is slot c of the block for node peer m; two lookups of one device share a slot exactly when they read the same table row. `group_slot`: entry u * 2 + k is slot k of the block for outer peer u; the entries of one device for one sending peer n are distinct; slots that carry no lookup name an arbitrary entry. `owner_row`: within one device and one sending peer the rows of different slots differ; slots that carry no lookup name an arbitrary row.
All inputs are finite; a program needn't handle non-finite values.
Results may differ from a plain program's by a relative error of at most 0.001.
Values may be sent and summed in bfloat16 or wider, within the bound.
A program may use at most 32 MiB of HBM per device.

v0:
```python
import jax
import jax.numpy as jnp
from jax import lax
from jax.sharding import PartitionSpec as P

learn_rate = 0.3


def indicator(values, columns, out_type):
    return (values[:, None] == jnp.arange(columns, dtype=jnp.int32)[None, :]).astype(out_type)


def bag_index(lengths, lookups):
    bag_ends = jnp.cumsum(lengths)
    places = jnp.arange(lookups, dtype=jnp.int32)
    return jnp.sum((places[:, None] >= bag_ends[None, :]).astype(jnp.int32), axis=1)


def slot_counts(slot_row, length_row, slot_span):
    lookups = slot_row.shape[0]
    bag_count = length_row.shape[0]
    return jnp.einsum(
        "ls,lb->sb",
        indicator(slot_row, slot_span, jnp.bfloat16),
        indicator(bag_index(length_row, lookups), bag_count, jnp.bfloat16),
        preferred_element_type=jnp.float32,
    )


def on_device(bag_grads, bag_lengths, look_slot, group_slot, owner_row, table, accum):
    groups = lax.axis_size("outer")
    members = lax.axis_size("node")
    cap_one = group_slot.shape[2]
    cap_two = owner_row.shape[2]
    row_width = table.shape[1]
    lookup_slot = look_slot[0]
    lengths = bag_lengths[0]
    group_map = group_slot[0].reshape(members * cap_one)
    counts = slot_counts(lookup_slot, lengths, members * cap_one)
    routed = jnp.dot(
        counts, bag_grads, precision=lax.Precision.HIGHEST, preferred_element_type=jnp.float32
    ).reshape(members, cap_one, row_width)
    arrived = lax.all_to_all(routed, "node", split_axis=0, concat_axis=0, tiled=True).reshape(
        members * cap_one, row_width
    )
    forwarded = jnp.einsum(
        "ij,ie->je",
        indicator(group_map, groups * cap_two, jnp.float32),
        arrived,
        precision=lax.Precision.HIGHEST,
        preferred_element_type=jnp.float32,
    )
    landed = lax.all_to_all(
        forwarded.reshape(groups, cap_two, row_width),
        "outer",
        split_axis=0,
        concat_axis=0,
        tiled=True,
    )
    owner_rows = owner_row[0].reshape(groups * cap_two)
    row_grads = (
        jnp.zeros(table.shape, jnp.float32)
        .at[owner_rows]
        .add(landed.reshape(groups * cap_two, row_width))
    )
    new_accum = accum + jnp.mean(row_grads * row_grads, axis=1)
    new_table = table - learn_rate * row_grads / jnp.sqrt(new_accum)[:, None]
    serving = new_table.astype(jnp.bfloat16)
    picked = serving[owner_rows].reshape(groups, cap_two, row_width)
    returned = lax.all_to_all(picked, "outer", split_axis=0, concat_axis=0, tiled=True).reshape(
        groups * cap_two, row_width
    )
    sent_back = returned[group_map].reshape(members, cap_one, row_width)
    reached = lax.all_to_all(sent_back, "node", split_axis=0, concat_axis=0, tiled=True).reshape(
        members * cap_one, row_width
    )
    fresh_rows = reached[lookup_slot]
    return (new_table, new_accum, fresh_rows)


def solution(mesh):
    placed = (
        P(("outer", "node"), None),
        P(("outer", "node"), None),
        P(("outer", "node"), None),
        P(("outer", "node"), None, None),
        P(("outer", "node"), None, None),
        P(("outer", "node"), None),
        P(("outer", "node")),
    )
    return jax.shard_map(
        on_device,
        mesh=mesh,
        in_specs=placed,
        out_specs=(P(("outer", "node"), None), P(("outer", "node")), P(("outer", "node"), None)),
        check_vma=False,
    )
```

profile of v0, /device:TPU:1, one launch (start us, length us, event | category | flops | bytes accessed | tf_op | source)
XLA Modules:
  0.0 90.6 jit_solution(15793475348845438736)
XLA Ops:
  0.6 0.0 copy-start
  0.6 0.0 copy-start.6
  0.7 0.7 copy-done.6
  1.3 0.1 copy.18
  1.4 0.1 reduce-window.8
  1.5 0.1 reduce
  1.6 0.0 copy-start.4
  1.6 0.1 convert_reduce_fusion
  1.7 0.6 copy-done.4
  2.3 0.4 fusion
  2.6 0.0 copy-done
  2.6 1.0 %fusion.11 = f32[192,128]{1,0:T(8,128)} fusion(f32[192,32]{0,1:T(8,128)S(1)} %fusion, f32[32,128]{1,0:T(8,128)S(1)} %copy-done), kind=kOutput, calls=%fused_computation.29 | convolution fusion | flops 9437184 | bytes 139264 | tf_op jit(solution)/shard_map/dot_general | solution.py:40
  3.6 0.0 copy-start.2
  3.6 7.8 %all-to-all-start = ((f32[8,24,128]{2,1,0:T(8,128)}), f32[8,24,128]{2,1,0:T(8,128)S(1)}, u32[]{:S(2)}, u32[]{:S(2)}) async-start(f32[8,24,128]{2,1,0:T(8,128)} %bitcast.3), calls=%async_computation | async-start | bytes 196608 | tf_op jit(solution)/shard_map/all_to_all | solution.py:43
  11.4 0.0 copy-done.2
  11.4 0.1 eq.59
  11.5 0.0 copy-start.5
  11.5 0.1 reshape_squeeze.7
  11.6 0.6 copy-done.5
  12.2 0.1 copy.17
  12.3 0.1 reshape_squeeze.6
  12.4 6.5 %all-to-all-done = f32[8,24,128]{2,1,0:T(8,128)S(1)} async-done(((f32[8,24,128]{2,1,0:T(8,128)}), f32[8,24,128]{2,1,0:T(8,128)S(1)}, u32[]{:S(2)}, u32[]{:S(2)}) %all-to-all-start) | async-done | bytes 98336 | tf_op jit(solution)/shard_map/all_to_all | solution.py:43
  19.0 0.3 fusion.4
  19.3 0.7 copy.19
  20.0 20.6 %all-to-all-start.1 = ((f32[96,2,128]{2,1,0:T(2,128)}), f32[96,2,128]{2,1,0:T(2,128)S(1)}, u32[]{:S(2)}, u32[]{:S(2)}) async-start(f32[96,2,128]{2,1,0:T(2,128)} %copy.19), calls=%async_computation.1 | async-start | bytes 196608 | tf_op jit(solution)/shard_map/all_to_all | solution.py:53
  40.7 13.5 %all-to-all-done.1 = f32[96,2,128]{2,1,0:T(2,128)S(1)} async-done(((f32[96,2,128]{2,1,0:T(2,128)}), f32[96,2,128]{2,1,0:T(2,128)S(1)}, u32[]{:S(2)}, u32[]{:S(2)}) %all-to-all-start.1) | async-done | bytes 98336 | tf_op jit(solution)/shard_map/all_to_all | solution.py:53
  54.2 0.0 copy-start.1
  54.2 1.3 %scatter_custom_fusion = f32[1024,128]{1,0:T(8,128)S(1)} fusion(s32[192]{0:T(256)S(1)} %bitcast.25, f32[192,128]{1,0:T(8,128)S(1)} %bitcast.22, f32[]{:T(128)} %constant.7.clone.1), kind=kCustom, calls=%fused_computation.10 | custom fusion | flops 24576 | bytes 524292 | tf_op jit(solution)/shard_map/scatter-add | solution.py:64
  55.5 0.0 copy-start.3
  55.5 0.2 multiply_reduce_fusion
  55.8 0.5 copy-done.3
  56.2 0.6 fusion.10
  56.8 0.0 copy-done.1
  56.8 1.0 %fusion.9 = (bf16[1024,128]{1,0:T(8,128)(2,1)S(1)}, f32[1024,128]{1,0:T(8,128)}) fusion(f32[1024,128]{1,0:T(8,128)S(1)} %copy-done.1, f32[1024]{0:T(1024)S(1)} %get-tuple-element.5, f32[1024,128]{1,0:T(8,128)S(1)} %scatter_custom_fusion), kind=kLoop, calls=%fused_computation.27 | loop fusion | flops 524288 | bytes 1839104 | tf_op jit(solution)/shard_map/convert_element_type | solution.py:68
  57.8 1.4 %gather_fusion = bf16[192,128]{1,0:T(8,128)(2,1)} fusion(bf16[1024,128]{1,0:T(8,128)(2,1)S(1)} %get-tuple-element.3, s32[1024]{0:T(1024)S(1)} %pad_clamp_fusion.2), kind=kCustom, calls=%fused_computation | custom fusion | bytes 99072 | tf_op jit(solution)/shard_map/gather | solution.py:69
  59.2 5.5 %all-to-all-start.2 = ((bf16[96,2,128]{2,1,0:T(2,128)(2,1)}), bf16[96,2,128]{2,1,0:T(2,128)(2,1)S(1)}, u32[]{:S(2)}, u32[]{:S(2)}) async-start(bf16[96,2,128]{2,1,0:T(2,128)(2,1)} %bitcast.7), calls=%async_computation.2 | async-start | bytes 98304 | tf_op jit(solution)/shard_map/all_to_all | solution.py:70
  64.7 12.3 %all-to-all-done.2 = bf16[96,2,128]{2,1,0:T(2,128)(2,1)S(1)} async-done(((bf16[96,2,128]{2,1,0:T(2,128)(2,1)}), bf16[96,2,128]{2,1,0:T(2,128)(2,1)S(1)}, u32[]{:S(2)}, u32[]{:S(2)}) %all-to-all-start.2) | async-done | bytes 49184 | tf_op jit(solution)/shard_map/all_to_all | solution.py:70
  77.0 1.4 %gather_fusion.1 = bf16[192,128]{1,0:T(8,128)(2,1)} fusion(bf16[192,128]{1,0:T(8,128)(2,1)S(1)} %bitcast.20, s32[1024]{0:T(1024)S(1)} %pad_clamp_fusion.1), kind=kCustom, calls=%fused_computation.1 | custom fusion | bytes 99072 | tf_op jit(solution)/shard_map/gather | solution.py:73
  78.4 3.3 %all-to-all-start.3 = ((bf16[8,24,128]{2,1,0:T(8,128)(2,1)}), bf16[8,24,128]{2,1,0:T(8,128)(2,1)S(1)}, u32[]{:S(2)}, u32[]{:S(2)}) async-start(bf16[8,24,128]{2,1,0:T(8,128)(2,1)} %bitcast.10), calls=%async_computation.3 | async-start | bytes 98304 | tf_op jit(solution)/shard_map/all_to_all | solution.py:74
  81.8 7.0 %all-to-all-done.3 = bf16[8,24,128]{2,1,0:T(8,128)(2,1)S(1)} async-done(((bf16[8,24,128]{2,1,0:T(8,128)(2,1)}), bf16[8,24,128]{2,1,0:T(8,128)(2,1)S(1)}, u32[]{:S(2)}, u32[]{:S(2)}) %all-to-all-start.3) | async-done | bytes 49184 | tf_op jit(solution)/shard_map/all_to_all | solution.py:74
  88.7 1.9 %gather_fusion.2 = bf16[512,128]{1,0:T(8,128)(2,1)} fusion(bf16[192,128]{1,0:T(8,128)(2,1)S(1)} %bitcast.19, s32[1024]{0:T(1024)S(1)} %pad_clamp_fusion), kind=kCustom, calls=%fused_computation.2 | custom fusion | bytes 264192 | tf_op jit(solution)/shard_map/gather | solution.py:77
  (7 shorter events, 0.0 us)
Async XLA Ops:
  0.6 2.0 %copy-start = (f32[32,128]{1,0:T(8,128)S(1)}, f32[32,128]{1,0:T(8,128)}, u32[]{:S(2)}) copy-start(f32[32,128]{1,0:T(8,128)} %param.7) | copy-start | bytes 49156
  0.6 0.7 copy-start.6
  1.6 0.7 copy-start.4
  3.6 7.8 %copy-start.2 = (s32[1,8,24]{2,1,0:T(8,128)S(1)}, s32[1,8,24]{2,1,0:T(8,128)}, u32[]{:S(2)}) copy-start(s32[1,8,24]{2,1,0:T(8,128)} %param.10) | copy-start | bytes 2308
  3.6 15.4 %all-to-all-start = ((f32[8,24,128]{2,1,0:T(8,128)}), f32[8,24,128]{2,1,0:T(8,128)S(1)}, u32[]{:S(2)}, u32[]{:S(2)}) async-start(f32[8,24,128]{2,1,0:T(8,128)} %bitcast.3), calls=%async_computation | async-start | bytes 196608 | tf_op jit(solution)/shard_map/all_to_all | solution.py:43
  11.5 0.7 copy-start.5
  20.0 34.2 %all-to-all-start.1 = ((f32[96,2,128]{2,1,0:T(2,128)}), f32[96,2,128]{2,1,0:T(2,128)S(1)}, u32[]{:S(2)}, u32[]{:S(2)}) async-start(f32[96,2,128]{2,1,0:T(2,128)} %copy.19), calls=%async_computation.1 | async-start | bytes 196608 | tf_op jit(solution)/shard_map/all_to_all | solution.py:53
  54.2 2.6 %copy-start.1 = (f32[1024,128]{1,0:T(8,128)S(1)}, f32[1024,128]{1,0:T(8,128)}, u32[]{:S(2)}) copy-start(f32[1024,128]{1,0:T(8,128)} %param.12) | copy-start | bytes 1572868
  55.5 0.7 copy-start.3
  59.2 17.8 %all-to-all-start.2 = ((bf16[96,2,128]{2,1,0:T(2,128)(2,1)}), bf16[96,2,128]{2,1,0:T(2,128)(2,1)S(1)}, u32[]{:S(2)}, u32[]{:S(2)}) async-start(bf16[96,2,128]{2,1,0:T(2,128)(2,1)} %bitcast.7), calls=%async_computation.2 | async-start | bytes 98304 | tf_op jit(solution)/shard_map/all_to_all | solution.py:70
  78.4 10.3 %all-to-all-start.3 = ((bf16[8,24,128]{2,1,0:T(8,128)(2,1)}), bf16[8,24,128]{2,1,0:T(8,128)(2,1)S(1)}, u32[]{:S(2)}, u32[]{:S(2)}) async-start(bf16[8,24,128]{2,1,0:T(8,128)(2,1)} %bitcast.10), calls=%async_computation.3 | async-start | bytes 98304 | tf_op jit(solution)/shard_map/all_to_all | solution.py:74
where the time goes:
time: 91.1 us; the launch traced here: 90.6 us
  waiting for transfers between devices  39.3 us (43%)
  starting transfers between devices  37.2 us (41%)
  local copies, waits for them, and re-layouts  8.23 us (9%)
  other arithmetic  3.45 us (4%)
  matrix products  1.62 us (2%)
    all_to_all x1, starting transfers between devices, on_device(): lax.all_to_all(forwarded.reshape(groups, cap_two, row_width), 'outer', sp...  20.6 us
    all_to_all x1, waiting for transfers between devices, on_device(): lax.all_to_all(forwarded.reshape(groups, cap_two, row_width), 'outer', sp...  13.5 us
    all_to_all x1, waiting for transfers between devices, on_device(): lax.all_to_all(picked, 'outer', split_axis=0, concat_axis=0, tiled=True)  12.3 us
    all_to_all x1, starting transfers between devices, on_device(): lax.all_to_all(routed, 'node', split_axis=0, concat_axis=0, tiled=True)  7.78 us
    all_to_all x1, waiting for transfers between devices, on_device(): lax.all_to_all(sent_back, 'node', split_axis=0, concat_axis=0, tiled=True)  6.96 us
    all_to_all x1, waiting for transfers between devices, on_device(): lax.all_to_all(routed, 'node', split_axis=0, concat_axis=0, tiled=True)  6.55 us
    all_to_all x1, starting transfers between devices, on_device(): lax.all_to_all(picked, 'outer', split_axis=0, concat_axis=0, tiled=True)  5.48 us
    all_to_all x1, starting transfers between devices, on_device(): lax.all_to_all(sent_back, 'node', split_axis=0, concat_axis=0, tiled=True)  3.35 us
  transfers between devices with their start and end apart: 4, of which 4 were waited for; matrix products, arithmetic and copies ran while one was open for 0% of the time, Pallas kernels for 0%

commit v1 on v0

v1 whole, which is shorter than its diff:
```python
import functools

import jax
import jax.numpy as jnp
from jax import lax
from jax.experimental import pallas as pl
from jax.experimental.pallas import tpu as pltpu
from jax.sharding import PartitionSpec as P

learn_rate = 0.3
MESH = pl.DeviceIdType.MESH
GROUPS = 96
PLANES = 12
SIDES = 8
MEMBERS = 8
CAP1 = 24
PAD1 = 32
CAP2 = 2
ROWS = 1024
LOOKS = 512
BAGS = 32
WIDTH = 128
SLOTS = 192
F32 = jnp.float32
BF16 = jnp.bfloat16


def iota(shape, dim):
    return lax.broadcasted_iota(jnp.int32, shape, dim)


def hot(condition):
    return jnp.where(condition, 1.0, 0.0).astype(BF16)


def split3(value):
    high = value.astype(BF16)
    rest = value - high.astype(F32)
    middle = rest.astype(BF16)
    low = (rest - middle.astype(F32)).astype(BF16)
    return jnp.concatenate([high, middle, low], axis=1)


def mix(ones, value):
    parts = jnp.dot(ones, split3(value), preferred_element_type=F32)
    return parts[:, :WIDTH] + (parts[:, WIDTH : 2 * WIDTH] + parts[:, 2 * WIDTH :])


def kernel(
    grads_in,
    lengths_in,
    look_in,
    group_in,
    owner_in,
    table_in,
    accum_in,
    table_out,
    accum_out,
    fresh_out,
    grads,
    lengths,
    look,
    group,
    owner,
    table,
    accum,
    routed,
    arrived,
    forwarded,
    landed,
    picked,
    returned,
    back,
    reached,
    new_table,
    new_accum,
    fresh,
    load_sem,
    out_sem,
    own_sem,
    send_sem,
    recv_sem,
    plane_sem,
):
    o = lax.axis_index("outer")
    n = lax.axis_index("node")
    z = o // SIDES
    side = lax.rem(o, SIDES)
    loads = [
        pltpu.make_async_copy(source, target, load_sem.at[i])
        for i, (source, target) in enumerate(
            (
                (look_in, look),
                (lengths_in, lengths),
                (grads_in, grads),
                (group_in, group),
                (owner_in, owner),
                (accum_in, accum),
                (table_in, table),
            )
        )
    ]
    for load in loads:
        load.start()

    barrier = pltpu.get_barrier_semaphore()
    node_peers = [lax.rem(n + i, MEMBERS) for i in (4, 3, 5, 2, 6, 1, 7)]
    plane_peers = [lax.rem(z + i, PLANES) * SIDES + side for i in (6, 5, 7, 4, 8, 3, 9, 2, 10, 1, 11)]
    for p in node_peers:
        pl.semaphore_signal(barrier, 1, device_id={"node": p}, device_id_type=MESH)
    for p in plane_peers:
        pl.semaphore_signal(barrier, 1, device_id={"outer": p}, device_id_type=MESH)
    for i in range(1, SIDES):
        p = z * SIDES + lax.rem(side + i, SIDES)
        pl.semaphore_signal(barrier, 1, device_id={"outer": p}, device_id_type=MESH)

    loads[0].wait()
    loads[1].wait()
    loads[2].wait()
    before = jnp.where(iota((BAGS, BAGS), 1) <= iota((BAGS, BAGS), 0), lengths[...], 0)
    ends = jnp.sum(before, axis=1, keepdims=True)
    own = jnp.where(iota((BAGS, BAGS), 1) == iota((BAGS, BAGS), 0), lengths[...], 0)
    starts = ends - jnp.sum(own, axis=1, keepdims=True)
    place = iota((BAGS, LOOKS), 1)
    of_bag = hot((place >= starts) & (place < ends))
    of_slot = hot(iota((SLOTS, LOOKS), 0) == look[...])
    counts = lax.dot_general(of_slot, of_bag, (((1,), (1,)), ((), ())), preferred_element_type=F32)
    routed[...] = mix(counts.astype(BF16), grads[...]).reshape(MEMBERS, CAP1, WIDTH)

    pl.semaphore_wait(barrier, MEMBERS - 1 + PLANES - 1 + SIDES - 1)
    for p in node_peers:
        pltpu.make_async_remote_copy(
            routed.at[p], arrived.at[n], send_sem.at[0], recv_sem.at[0], device_id={"node": p}, device_id_type=MESH
        ).start()
    for p in plane_peers:
        pl.semaphore_signal(plane_sem, 1, device_id={"outer": p}, device_id_type=MESH)
    arrived[n] = routed[n]

    loads[3].wait()
    sender = lax.shift_right_logical(iota((MEMBERS, SLOTS), 1) * 2731, 16)
    column = lax.shift_right_logical(iota((CAP1, SLOTS), 1) * 2731, 16)
    spread = hot(iota((CAP1, SLOTS), 1) - CAP1 * column == iota((CAP1, SLOTS), 0))
    slots = jnp.dot(group[0].astype(F32).astype(BF16), spread, preferred_element_type=F32)
    group_row = jnp.sum(jnp.where(sender == iota((MEMBERS, SLOTS), 0), slots, 0.0), axis=0, keepdims=True).astype(jnp.int32)
    to_group = hot(iota((SLOTS, SLOTS), 0) == group_row)

    landing = arrived.at[pl.ds(0, MEMBERS - 1)]
    pltpu.make_async_copy(landing, landing, recv_sem.at[0]).wait()
    forwarded[...] = mix(to_group, arrived[...].reshape(SLOTS, WIDTH))
    pl.semaphore_wait(plane_sem, PLANES - 1)

    def outer_peer(i):
        return lax.rem(o + i, GROUPS)

    def exchange(source, target, index):
        def send(i, carry):
            p = outer_peer(i)
            pltpu.make_async_remote_copy(
                source.at[pl.ds(CAP2 * p, CAP2)],
                target.at[pl.ds(CAP2 * o, CAP2)],
                send_sem.at[index],
                recv_sem.at[index],
                device_id={"outer": p},
                device_id_type=MESH,
            ).start()
            return carry

        lax.fori_loop(1, GROUPS, send, 0, unroll=5)
        mine = pltpu.make_async_copy(
            source.at[pl.ds(CAP2 * o, CAP2)], target.at[pl.ds(CAP2 * o, CAP2)], own_sem.at[index - 1]
        )
        mine.start()
        return mine

    def rows_of(ref, rows):
        return ref.at[pl.ds(0, rows)]

    def wait_bytes(part, semaphore):
        pltpu.make_async_copy(part, part, semaphore).wait()

    mine_forward = exchange(forwarded, landed, 1)

    loads[4].wait()
    loads[5].wait()
    loads[6].wait()
    owner_high = lax.shift_right_logical(owner[0], 5)
    owner_low = owner[0] - 32 * owner_high
    digits = jnp.concatenate([owner_high, owner_low], axis=0).astype(F32).astype(BF16)
    pair = hot(lax.shift_right_logical(iota((GROUPS, SLOTS), 1), 1) == iota((GROUPS, SLOTS), 0))
    laid = jnp.dot(digits, pair, preferred_element_type=F32)
    even = (iota((1, SLOTS), 1) & 1) == 0
    owner_row = 32.0 * jnp.where(even, laid[0:1], laid[1:2]) + jnp.where(even, laid[2:3], laid[3:4])
    owner_row = owner_row.astype(jnp.int32)
    diagonal = iota((SLOTS, SLOTS), 0) == iota((SLOTS, SLOTS), 1)
    owner_column = jnp.sum(jnp.where(diagonal, owner_row, 0), axis=1, keepdims=True)
    same_row = hot(owner_column == owner_row)
    to_row = hot(iota((ROWS, SLOTS), 0) == owner_row)
    from_row = hot(owner_column == iota((SLOTS, ROWS), 1))
    old_rows = mix(from_row, table[...])
    by_lane = jnp.where((owner_column & 127) == iota((SLOTS, WIDTH), 1), 1.0, 0.0)
    by_block = lax.shift_right_logical(owner_column, 7)
    chosen = jnp.zeros((SLOTS, WIDTH), F32)
    for a in range(ROWS // WIDTH):
        chosen = jnp.where(by_block == a, accum[a : a + 1, :], chosen)
    old_accum = jnp.sum(chosen * by_lane, axis=1, keepdims=True)

    padded = iota((MEMBERS * PAD1, SLOTS), 0)
    slot_place = iota((MEMBERS * PAD1, SLOTS), 1)
    spaced = hot(slot_place + 8 * lax.shift_right_logical(slot_place * 2731, 16) == padded)
    from_group = lax.dot_general(spaced, to_group, (((1,), (1,)), ((), ())), preferred_element_type=F32).astype(BF16)
    look_spaced = look[...] + 8 * lax.shift_right_logical(look[...] * 2731, 16)
    look_hot = hot(iota((MEMBERS * PAD1, LOOKS), 0) == look_spaced)
    eye = hot(iota((LOOKS, LOOKS), 0) == iota((LOOKS, LOOKS), 1))
    from_look = lax.dot_general(eye, look_hot, (((1,), (1,)), ((), ())), preferred_element_type=F32).astype(BF16)

    mine_forward.wait()
    wait_bytes(rows_of(landed, SLOTS - CAP2), recv_sem.at[1])
    came = split3(landed[...])
    sums = jnp.dot(same_row, came, preferred_element_type=F32)
    slot_grads = sums[:, :WIDTH] + (sums[:, WIDTH : 2 * WIDTH] + sums[:, 2 * WIDTH :])
    slot_accum = old_accum + jnp.mean(slot_grads * slot_grads, axis=1, keepdims=True)
    fresh_slots = old_rows - learn_rate * slot_grads / jnp.sqrt(slot_accum)
    picked[...] = fresh_slots.astype(BF16).astype(F32)
    mine_picked = exchange(picked, returned, 2)

    turned = jnp.transpose(jnp.concatenate([accum[...]] * (WIDTH // 8), axis=0))
    next_accum = jnp.zeros((WIDTH, WIDTH), F32)
    lane = iota((WIDTH, WIDTH), 1)
    for a in range(ROWS // WIDTH):
        part = slice(a * WIDTH, (a + 1) * WIDTH)
        sums = jnp.dot(to_row[part], came, preferred_element_type=F32)
        row_grads = sums[:, :WIDTH] + (sums[:, WIDTH : 2 * WIDTH] + sums[:, 2 * WIDTH :])
        row_accum = turned[:, a : a + 1] + jnp.mean(row_grads * row_grads, axis=1, keepdims=True)
        new_table[part, :] = table[part, :] - learn_rate * row_grads / jnp.sqrt(row_accum)
        next_accum = jnp.where(lane == a, row_accum, next_accum)
    new_accum[...] = jnp.transpose(next_accum)[: ROWS // WIDTH]
    table_copy = pltpu.make_async_copy(new_table, table_out, out_sem.at[0])
    table_copy.start()
    accum_copy = pltpu.make_async_copy(new_accum, accum_out, out_sem.at[1])
    accum_copy.start()

    mine_picked.wait()
    wait_bytes(rows_of(returned, SLOTS - CAP2), recv_sem.at[2])
    gathered = jnp.dot(from_group, returned[...].astype(BF16), preferred_element_type=F32)
    back[...] = gathered.astype(BF16).reshape(MEMBERS, PAD1, WIDTH)
    for p in node_peers:
        pltpu.make_async_remote_copy(
            back.at[p], reached.at[n], send_sem.at[3], recv_sem.at[3], device_id={"node": p}, device_id_type=MESH
        ).start()
    reached[n] = back[n]

    landing = reached.at[pl.ds(0, MEMBERS - 1)]
    wait_bytes(landing, recv_sem.at[3])
    read = jnp.dot(from_look, reached[...].reshape(MEMBERS * PAD1, WIDTH), preferred_element_type=F32)
    fresh[...] = read.astype(BF16)
    fresh_copy = pltpu.make_async_copy(fresh, fresh_out, out_sem.at[2])
    fresh_copy.start()

    wait_bytes(routed.at[pl.ds(0, MEMBERS - 1)], send_sem.at[0])
    wait_bytes(rows_of(forwarded, SLOTS - CAP2), send_sem.at[1])
    wait_bytes(rows_of(picked, SLOTS - CAP2), send_sem.at[2])
    wait_bytes(back.at[pl.ds(0, MEMBERS - 1)], send_sem.at[3])
    table_copy.wait()
    accum_copy.wait()
    fresh_copy.wait()


def on_device(bag_grads, bag_lengths, look_slot, group_slot, owner_row, table, accum):
    outs = pl.pallas_call(
        kernel,
        out_shape=(
            jax.ShapeDtypeStruct((ROWS, WIDTH), F32),
            jax.ShapeDtypeStruct((ROWS // WIDTH, WIDTH), F32),
            jax.ShapeDtypeStruct((LOOKS, WIDTH), BF16),
        ),
        in_specs=[pl.BlockSpec(memory_space=pltpu.HBM)] * 7,
        out_specs=[pl.BlockSpec(memory_space=pltpu.HBM)] * 3,
        scratch_shapes=[
            pltpu.VMEM((BAGS, WIDTH), F32),
            pltpu.VMEM((1, BAGS), jnp.int32),
            pltpu.VMEM((1, LOOKS), jnp.int32),
            pltpu.VMEM((1, MEMBERS, CAP1), jnp.int32),
            pltpu.VMEM((1, CAP2, GROUPS), jnp.int32),
            pltpu.VMEM((ROWS, WIDTH), F32),
            pltpu.VMEM((ROWS // WIDTH, WIDTH), F32),
            pltpu.VMEM((MEMBERS, CAP1, WIDTH), F32),
            pltpu.VMEM((MEMBERS, CAP1, WIDTH), F32),
            pltpu.VMEM((SLOTS, WIDTH), F32),
            pltpu.VMEM((SLOTS, WIDTH), F32),
            pltpu.VMEM((SLOTS, WIDTH), F32),
            pltpu.VMEM((SLOTS, WIDTH), F32),
            pltpu.VMEM((MEMBERS, PAD1, WIDTH), BF16),
            pltpu.VMEM((MEMBERS, PAD1, WIDTH), BF16),
            pltpu.VMEM((ROWS, WIDTH), F32),
            pltpu.VMEM((ROWS // WIDTH, WIDTH), F32),
            pltpu.VMEM((LOOKS, WIDTH), BF16),
            pltpu.SemaphoreType.DMA((7,)),
            pltpu.SemaphoreType.DMA((3,)),
            pltpu.SemaphoreType.DMA((2,)),
            pltpu.SemaphoreType.DMA((4,)),
            pltpu.SemaphoreType.DMA((4,)),
            pltpu.SemaphoreType.REGULAR,
        ],
        compiler_params=pltpu.CompilerParams(collective_id=0, has_side_effects=True, vmem_limit_bytes=32 * 1024 * 1024),
        cost_estimate=pl.CostEstimate(flops=600_000_000, bytes_accessed=1_400_000, transcendentals=1024),
    )(
        bag_grads,
        bag_lengths,
        look_slot,
        group_slot,
        jnp.transpose(owner_row, (0, 2, 1)),
        table,
        accum.reshape(ROWS // WIDTH, WIDTH),
    )
    return outs[0], outs[1].reshape(ROWS), outs[2]


def solution(mesh):
    both = ("outer", "node")
    placed = (
        P(both, None),
        P(both, None),
        P(both, None),
        P(both, None, None),
        P(both, None, None),
        P(both, None),
        P(both),
    )
    return jax.shard_map(
        on_device,
        mesh=mesh,
        in_specs=placed,
        out_specs=(P(both, None), P(both), P(both, None)),
        check_vma=False,
    )
```

time: 91.1 us -> 53.1 us (0.58)
  Pallas kernels: 0 us -> 46.2 us
  waiting for transfers between devices: 39.3 us -> 0 us
  starting transfers between devices: 37.2 us -> 0 us
  other arithmetic: 3.45 us -> 0 us
  local copies, waits for them, and re-layouts: 8.23 us -> 5.85 us
  matrix products: 1.62 us -> 0 us
    pallas_call x0 -> x1, Pallas kernels: none -> 46.2 us  [on_device(): pl.pallas_call(kernel, out_shape=(jax.ShapeDtypeStruct((ROWS, WIDTH), F32...]
    all_to_all x4 -> x0, waiting for transfers between devices: 39.3 us -> none  [the longest x1 13.5 us: on_device(): lax.all_to_all(forwarded.reshape(groups, cap_two, row_width), 'outer', sp...]
    all_to_all x4 -> x0, starting transfers between devices: 37.2 us -> none  [the longest x1 20.6 us: on_device(): lax.all_to_all(forwarded.reshape(groups, cap_two, row_width), 'outer', sp...]
    gather x3 -> x0, local copies, waits for them, and re-layouts: 4.69 us -> none  [the longest x1 1.91 us: on_device(): fresh_rows = reached[lookup_slot]]
    unnamed x15 -> x17, local copies, waits for them, and re-layouts: 2.44 us -> 5.85 us
    dot_general x3 -> x0, matrix products: 1.62 us -> none  [the longest x1 0.98 us: on_device(): jnp.dot(counts, bag_grads, precision=lax.Precision.HIGHEST, preferred_ele...]
    scatter-add x1 -> x0, other arithmetic: 1.35 us -> none  [on_device(): row_grads = jnp.zeros(table.shape, jnp.float32).at[owner_rows].add(landed...]
    convert_element_type x1 -> x0, other arithmetic: 1 us -> none  [on_device(): serving = new_table.astype(jnp.bfloat16)]
  transfers between devices with their start and end apart: 4 -> 0, of which waited for: 4 -> 0; matrix products, arithmetic and copies ran while one was open for 0% -> 0% of each run, Pallas kernels for 0% -> 0%
where the time goes in v1:
time: 53.1 us; the launch traced here: 52.8 us
  Pallas kernels  46.2 us (87%)
  local copies, waits for them, and re-layouts  5.85 us (11%)
  between operations  0.67 us (1%)
    pallas_call x1, Pallas kernels, on_device(): pl.pallas_call(kernel, out_shape=(jax.ShapeDtypeStruct((ROWS, WIDTH), F32...  46.2 us
    unnamed x17, local copies, waits for them, and re-layouts  5.85 us

profile of v1, /device:TPU:1, one launch (start us, length us, event | category | flops | bytes accessed | tf_op | source)
XLA Modules:
  0.0 52.8 jit_solution(14835790741793838692)
XLA Ops:
  0.6 0.0 copy-start.4
  0.6 0.0 copy-start.5
  0.7 0.0 copy-start.6
  0.7 0.7 %copy-done.4 = s32[1,512]{1,0:T(1,128)S(1)} copy-done((s32[1,512]{1,0:T(1,128)S(1)}, s32[1,512]{1,0:T(1,128)}, u32[]{:S(2)}) %copy-start.4) | copy-done | bytes 2072
  1.3 0.0 copy-done.5
  1.3 0.0 copy-done.6
  1.3 0.0 copy-start
  1.3 1.0 %copy-done = f32[1024,128]{1,0:T(8,128)S(1)} copy-done((f32[1024,128]{1,0:T(8,128)S(1)}, f32[1024,128]{1,0:T(8,128)}, u32[]{:S(2)}) %copy-start) | copy-done | bytes 524312
  2.4 0.0 copy-start.1
  2.4 0.7 %copy-done.1 = f32[32,128]{1,0:T(8,128)S(1)} copy-done((f32[32,128]{1,0:T(8,128)S(1)}, f32[32,128]{1,0:T(8,128)}, u32[]{:S(2)}) %copy-start.1) | copy-done | bytes 16408
  3.1 0.0 copy-start.2
  3.1 0.7 %copy-done.2 = s32[1,8,24]{2,1,0:T(8,128)S(1)} copy-done((s32[1,8,24]{2,1,0:T(8,128)S(1)}, s32[1,8,24]{2,1,0:T(8,128)}, u32[]{:S(2)}) %copy-start.2) | copy-done | bytes 792
  3.8 0.0 copy-start.3
  3.8 0.7 %copy-done.3 = f32[1024]{0:T(1024)S(1)} copy-done((f32[1024]{0:T(1024)S(1)}, f32[1024]{0:T(1024)}, u32[]{:S(2)}) %copy-start.3) | copy-done | bytes 4120
  4.5 46.2 %shard_map.94 = (f32[1024,128]{1,0:T(8,128)S(1)}, f32[8,128]{1,0:T(8,128)S(1)}, bf16[512,128]{1,0:T(8,128)(2,1)S(1)}) custom-call(f32[32,128]{1,0:T(8,128)S(1)} %copy-done.1, s32[1,32]{1,0:T(1,128)S(1)} %copy-done.6, s32[1,512]{1,0:T(1,128)S(1)} %copy-done.4, s32[1,8,24]{2,1,0:T(8,128)S(1)} %copy-done.2, s32[1,2,96]{2,1,0:T(2,128)S(1)} %bitcast.5, ...), custom_call_target="tpu_custom_call" | custom-call | flops 600000000 | bytes 1400000 | tf_op jit(solution)/shard_map/pallas_call | solution.py:269
  50.7 0.8 %copy.13 = f32[1024,128]{1,0:T(8,128)} copy(f32[1024,128]{1,0:T(8,128)S(1)} %get-tuple-element.12) | data formatting | bytes 1048576
  51.5 0.6 %copy.14 = f32[1024]{0:T(1024)} copy(f32[1024]{0:T(1024)S(1)} %bitcast.3) | data formatting | bytes 8192
  52.1 0.7 %copy.15 = bf16[512,128]{1,0:T(8,128)(2,1)} copy(bf16[512,128]{1,0:T(8,128)(2,1)S(1)} %get-tuple-element.14) | data formatting | bytes 262144
Async XLA Ops:
  0.6 0.7 %copy-start.4 = (s32[1,512]{1,0:T(1,128)S(1)}, s32[1,512]{1,0:T(1,128)}, u32[]{:S(2)}) copy-start(s32[1,512]{1,0:T(1,128)} %look_in.1) | copy-start | bytes 6148
  0.6 0.7 %copy-start.5 = (s32[1,96,2]{1,2,0:T(2,128)S(1)}, s32[1,96,2]{1,2,0:T(2,128)}, u32[]{:S(2)}) copy-start(s32[1,96,2]{1,2,0:T(2,128)} %param.11) | copy-start | bytes 2308
  0.7 0.7 %copy-start.6 = (s32[1,32]{1,0:T(1,128)S(1)}, s32[1,32]{1,0:T(1,128)}, u32[]{:S(2)}) copy-start(s32[1,32]{1,0:T(1,128)} %lengths_in.1) | copy-start | bytes 388
  1.3 1.0 %copy-start = (f32[1024,128]{1,0:T(8,128)S(1)}, f32[1024,128]{1,0:T(8,128)}, u32[]{:S(2)}) copy-start(f32[1024,128]{1,0:T(8,128)} %table_in.1) | copy-start | bytes 1572868
  2.4 0.7 %copy-start.1 = (f32[32,128]{1,0:T(8,128)S(1)}, f32[32,128]{1,0:T(8,128)}, u32[]{:S(2)}) copy-start(f32[32,128]{1,0:T(8,128)} %grads_in.1) | copy-start | bytes 49156
  3.1 0.7 %copy-start.2 = (s32[1,8,24]{2,1,0:T(8,128)S(1)}, s32[1,8,24]{2,1,0:T(8,128)}, u32[]{:S(2)}) copy-start(s32[1,8,24]{2,1,0:T(8,128)} %group_in.1) | copy-start | bytes 2308
  3.8 0.7 %copy-start.3 = (f32[1024]{0:T(1024)S(1)}, f32[1024]{0:T(1024)}, u32[]{:S(2)}) copy-start(f32[1024]{0:T(1024)} %param.13) | copy-start | bytes 12292

commit v2 on v1

--- a/solution.py
+++ b/solution.py
@@ -10,6 +10,7 @@
 learn_rate = 0.3
 MESH = pl.DeviceIdType.MESH
 GROUPS = 96
+FAR_FIRST = (6, 5, 7, 4, 8, 3, 9, 2, 10, 1, 11, 0)
 PLANES = 12
 SIDES = 8
 MEMBERS = 8
@@ -54,9 +55,9 @@
     owner_in,
     table_in,
     accum_in,
-    table_out,
-    accum_out,
-    fresh_out,
+    new_table,
+    new_accum,
+    fresh,
     grads,
     lengths,
     look,
@@ -72,11 +73,7 @@
     returned,
     back,
     reached,
-    new_table,
-    new_accum,
-    fresh,
     load_sem,
-    out_sem,
     own_sem,
     send_sem,
     recv_sem,
@@ -149,23 +146,23 @@
     forwarded[...] = mix(to_group, arrived[...].reshape(SLOTS, WIDTH))
     pl.semaphore_wait(plane_sem, PLANES - 1)
 
-    def outer_peer(i):
-        return lax.rem(o + i, GROUPS)
-
-    def exchange(source, target, index):
-        def send(i, carry):
-            p = outer_peer(i)
-            pltpu.make_async_remote_copy(
-                source.at[pl.ds(CAP2 * p, CAP2)],
-                target.at[pl.ds(CAP2 * o, CAP2)],
-                send_sem.at[index],
-                recv_sem.at[index],
-                device_id={"outer": p},
-                device_id_type=MESH,
-            ).start()
-            return carry
-
-        lax.fori_loop(1, GROUPS, send, 0, unroll=5)
+    def exchange(source, target, index, order):
+        for away in order:
+            plane = lax.rem(z + away, PLANES) * SIDES
+
+            def send(i, carry, plane=plane):
+                p = plane + lax.rem(side + i, SIDES)
+                pltpu.make_async_remote_copy(
+                    source.at[pl.ds(CAP2 * p, CAP2)],
+                    target.at[pl.ds(CAP2 * o, CAP2)],
+                    send_sem.at[index],
+                    recv_sem.at[index],
+                    device_id={"outer": p},
+                    device_id_type=MESH,
+                ).start()
+                return carry
+
+            lax.fori_loop(1 if away == 0 else 0, SIDES, send, 0, unroll=7 if away == 0 else 8)
         mine = pltpu.make_async_copy(
             source.at[pl.ds(CAP2 * o, CAP2)], target.at[pl.ds(CAP2 * o, CAP2)], own_sem.at[index - 1]
         )
@@ -178,7 +175,7 @@
     def wait_bytes(part, semaphore):
         pltpu.make_async_copy(part, part, semaphore).wait()
 
-    mine_forward = exchange(forwarded, landed, 1)
+    mine_forward = exchange(forwarded, landed, 1, FAR_FIRST)
 
     loads[4].wait()
     loads[5].wait()
@@ -221,7 +218,7 @@
     slot_accum = old_accum + jnp.mean(slot_grads * slot_grads, axis=1, keepdims=True)
     fresh_slots = old_rows - learn_rate * slot_grads / jnp.sqrt(slot_accum)
     picked[...] = fresh_slots.astype(BF16).astype(F32)
-    mine_picked = exchange(picked, returned, 2)
+    mine_picked = exchange(picked, returned, 2, FAR_FIRST)
 
     turned = jnp.transpose(jnp.concatenate([accum[...]] * (WIDTH // 8), axis=0))
     next_accum = jnp.zeros((WIDTH, WIDTH), F32)
@@ -234,10 +231,6 @@
         new_table[part, :] = table[part, :] - learn_rate * row_grads / jnp.sqrt(row_accum)
         next_accum = jnp.where(lane == a, row_accum, next_accum)
     new_accum[...] = jnp.transpose(next_accum)[: ROWS // WIDTH]
-    table_copy = pltpu.make_async_copy(new_table, table_out, out_sem.at[0])
-    table_copy.start()
-    accum_copy = pltpu.make_async_copy(new_accum, accum_out, out_sem.at[1])
-    accum_copy.start()
 
     mine_picked.wait()
     wait_bytes(rows_of(returned, SLOTS - CAP2), recv_sem.at[2])
@@ -253,16 +246,22 @@
     wait_bytes(landing, recv_sem.at[3])
     read = jnp.dot(from_look, reached[...].reshape(MEMBERS * PAD1, WIDTH), preferred_element_type=F32)
     fresh[...] = read.astype(BF16)
-    fresh_copy = pltpu.make_async_copy(fresh, fresh_out, out_sem.at[2])
-    fresh_copy.start()
 
     wait_bytes(routed.at[pl.ds(0, MEMBERS - 1)], send_sem.at[0])
     wait_bytes(rows_of(forwarded, SLOTS - CAP2), send_sem.at[1])
     wait_bytes(rows_of(picked, SLOTS - CAP2), send_sem.at[2])
     wait_bytes(back.at[pl.ds(0, MEMBERS - 1)], send_sem.at[3])
-    table_copy.wait()
-    accum_copy.wait()
-    fresh_copy.wait()
+
+
+def hand_over(table, accum, fresh, table_out, accum_out, fresh_out, sem):
+    copies = [
+        pltpu.make_async_copy(source, target, sem.at[i])
+        for i, (source, target) in enumerate(((table, table_out), (fresh, fresh_out), (accum, accum_out)))
+    ]
+    for copy in copies:
+        copy.start()
+    for copy in copies:
+        copy.wait()
 
 
 def on_device(bag_grads, bag_lengths, look_slot, group_slot, owner_row, table, accum):
@@ -274,7 +273,7 @@
             jax.ShapeDtypeStruct((LOOKS, WIDTH), BF16),
         ),
         in_specs=[pl.BlockSpec(memory_space=pltpu.HBM)] * 7,
-        out_specs=[pl.BlockSpec(memory_space=pltpu.HBM)] * 3,
+        out_specs=[pl.BlockSpec(memory_space=pltpu.VMEM)] * 3,
         scratch_shapes=[
             pltpu.VMEM((BAGS, WIDTH), F32),
             pltpu.VMEM((1, BAGS), jnp.int32),
@@ -291,11 +290,7 @@
             pltpu.VMEM((SLOTS, WIDTH), F32),
             pltpu.VMEM((MEMBERS, PAD1, WIDTH), BF16),
             pltpu.VMEM((MEMBERS, PAD1, WIDTH), BF16),
-            pltpu.VMEM((ROWS, WIDTH), F32),
-            pltpu.VMEM((ROWS // WIDTH, WIDTH), F32),
-            pltpu.VMEM((LOOKS, WIDTH), BF16),
             pltpu.SemaphoreType.DMA((7,)),
-            pltpu.SemaphoreType.DMA((3,)),
             pltpu.SemaphoreType.DMA((2,)),
             pltpu.SemaphoreType.DMA((4,)),
             pltpu.SemaphoreType.DMA((4,)),
@@ -304,15 +299,18 @@
         compiler_params=pltpu.CompilerParams(collective_id=0, has_side_effects=True, vmem_limit_bytes=32 * 1024 * 1024),
         cost_estimate=pl.CostEstimate(flops=600_000_000, bytes_accessed=1_400_000, transcendentals=1024),
     )(
-        bag_grads,
-        bag_lengths,
-        look_slot,
-        group_slot,
-        jnp.transpose(owner_row, (0, 2, 1)),
-        table,
-        accum.reshape(ROWS // WIDTH, WIDTH),
+        *[pltpu.with_memory_space_constraint(a, pltpu.HBM) for a in (bag_grads, bag_lengths, look_slot, group_slot, jnp.transpose(owner_row, (0, 2, 1)), table, accum.reshape(ROWS // WIDTH, WIDTH))]
     )
-    return outs[0], outs[1].reshape(ROWS), outs[2]
+    table, accum, fresh = pl.pallas_call(
+        hand_over,
+        out_shape=[jax.ShapeDtypeStruct(out.shape, out.dtype) for out in outs],
+        in_specs=[pl.BlockSpec(memory_space=pltpu.VMEM)] * 3,
+        out_specs=[pl.BlockSpec(memory_space=pltpu.HBM)] * 3,
+        scratch_shapes=[pltpu.SemaphoreType.DMA((3,))],
+        compiler_params=pltpu.CompilerParams(vmem_limit_bytes=16 * 1024 * 1024),
+        cost_estimate=pl.CostEstimate(flops=0, bytes_accessed=1_400_000, transcendentals=0),
+    )(*outs)
+    return table, accum.reshape(ROWS), fresh
 
 
 def solution(mesh):

time: 53.1 us -> 46.3 us (0.87)
  local copies, waits for them, and re-layouts: 5.85 us -> 0 us
  Pallas kernels: 46.2 us -> 45.5 us
    unnamed x17 -> x0, local copies, waits for them, and re-layouts: 5.85 us -> none
    pallas_call x1, Pallas kernels: 46.2 us -> 44.7 us  [on_device(): pl.pallas_call(kernel, out_shape=(jax.ShapeDtypeStruct((ROWS, WIDTH), F32...]
    pallas_call x0 -> x1, Pallas kernels: none -> 0.86 us  [on_device(): pl.pallas_call(hand_over, out_shape=[jax.ShapeDtypeStruct(out.shape, out....]
where the time goes in v2:
time: 46.3 us; the launch traced here: 46.2 us
  Pallas kernels  45.5 us (98%)
  between operations  0.64 us (1%)
    pallas_call x1, Pallas kernels, on_device(): pl.pallas_call(kernel, out_shape=(jax.ShapeDtypeStruct((ROWS, WIDTH), F32...  44.7 us

profile of v2, /device:TPU:1, one launch (start us, length us, event | category | flops | bytes accessed | tf_op | source)
XLA Modules:
  0.0 46.2 jit_solution(5151642241719576711)
XLA Ops:
  0.6 44.7 %shard_map.94 = (f32[1024,128]{1,0:T(8,128)S(1)}, f32[8,128]{1,0:T(8,128)S(1)}, bf16[512,128]{1,0:T(8,128)(2,1)S(1)}) custom-call(f32[32,128]{1,0:T(8,128)} %grads_in.1, s32[1,32]{1,0:T(1,128)} %lengths_in.1, s32[1,512]{1,0:T(1,128)} %look_in.1, s32[1,8,24]{2,1,0:T(8,128)} %group_in.1, s32[1,2,96]{2,1,0:T(2,128)} %bitcast.5, f32[1024,128]{1,0:T(8,128)} %table_in.1, ...), custom_call_target="tpu_custom_call" | custom-call | flops 600000000 | bytes 1400000 | tf_op jit(solution)/shard_map/pallas_call | solution.py:268
  45.3 0.9 %shard_map.95 = (f32[1024,128]{1,0:T(8,128)}, f32[8,128]{1,0:T(8,128)}, bf16[512,128]{1,0:T(8,128)(2,1)}) custom-call(f32[1024,128]{1,0:T(8,128)S(1)} %get-tuple-element.9.table, f32[8,128]{1,0:T(8,128)S(1)} %get-tuple-element.10.accum, bf16[512,128]{1,0:T(8,128)(2,1)S(1)} %get-tuple-element.11.fresh), custom_call_target="tpu_custom_call" | custom-call | bytes 1400000 | tf_op jit(solution)/shard_map/pallas_call | solution.py:304

commit v3 on v2

--- a/solution.py
+++ b/solution.py
@@ -10,7 +10,8 @@
 learn_rate = 0.3
 MESH = pl.DeviceIdType.MESH
 GROUPS = 96
-FAR_FIRST = (6, 5, 7, 4, 8, 3, 9, 2, 10, 1, 11, 0)
+FROM_FAR = (6, 5, 7, 4, 8, 3, 9, 2, 10, 1, 11, 0)
+FROM_NEAR = (0, 1, 2, 3, 4, 5, 6, 7, 8, 9, 10, 11)
 PLANES = 12
 SIDES = 8
 MEMBERS = 8
@@ -57,7 +58,8 @@
     accum_in,
     new_table,
     new_accum,
-    fresh,
+    from_look,
+    reached,
     grads,
     lengths,
     look,
@@ -72,12 +74,11 @@
     picked,
     returned,
     back,
-    reached,
     load_sem,
     own_sem,
     send_sem,
     recv_sem,
-    plane_sem,
+    side_sem,
 ):
     o = lax.axis_index("outer")
     n = lax.axis_index("node")
@@ -103,12 +104,12 @@
     barrier = pltpu.get_barrier_semaphore()
     node_peers = [lax.rem(n + i, MEMBERS) for i in (4, 3, 5, 2, 6, 1, 7)]
     plane_peers = [lax.rem(z + i, PLANES) * SIDES + side for i in (6, 5, 7, 4, 8, 3, 9, 2, 10, 1, 11)]
+    side_peers = [z * SIDES + lax.rem(side + i, SIDES) for i in (4, 3, 5, 2, 6, 1, 7)]
     for p in node_peers:
         pl.semaphore_signal(barrier, 1, device_id={"node": p}, device_id_type=MESH)
     for p in plane_peers:
         pl.semaphore_signal(barrier, 1, device_id={"outer": p}, device_id_type=MESH)
-    for i in range(1, SIDES):
-        p = z * SIDES + lax.rem(side + i, SIDES)
+    for p in side_peers:
         pl.semaphore_signal(barrier, 1, device_id={"outer": p}, device_id_type=MESH)
 
     loads[0].wait()
@@ -129,8 +130,8 @@
         pltpu.make_async_remote_copy(
             routed.at[p], arrived.at[n], send_sem.at[0], recv_sem.at[0], device_id={"node": p}, device_id_type=MESH
         ).start()
-    for p in plane_peers:
-        pl.semaphore_signal(plane_sem, 1, device_id={"outer": p}, device_id_type=MESH)
+    for p in side_peers:
+        pl.semaphore_signal(side_sem, 1, device_id={"outer": p}, device_id_type=MESH)
     arrived[n] = routed[n]
 
     loads[3].wait()
@@ -144,17 +145,20 @@
     landing = arrived.at[pl.ds(0, MEMBERS - 1)]
     pltpu.make_async_copy(landing, landing, recv_sem.at[0]).wait()
     forwarded[...] = mix(to_group, arrived[...].reshape(SLOTS, WIDTH))
-    pl.semaphore_wait(plane_sem, PLANES - 1)
+    pl.semaphore_wait(side_sem, SIDES - 1)
+
+    def block(ref, group):
+        return ref.at[pl.ds(CAP2 * group, CAP2)] if len(ref.shape) == 2 else ref.at[group]
 
     def exchange(source, target, index, order):
-        for away in order:
-            plane = lax.rem(z + away, PLANES) * SIDES
+        for place_z in order:
+            plane = place_z * SIDES
 
             def send(i, carry, plane=plane):
                 p = plane + lax.rem(side + i, SIDES)
                 pltpu.make_async_remote_copy(
-                    source.at[pl.ds(CAP2 * p, CAP2)],
-                    target.at[pl.ds(CAP2 * o, CAP2)],
+                    block(source, p),
+                    block(target, o),
                     send_sem.at[index],
                     recv_sem.at[index],
                     device_id={"outer": p},
@@ -162,9 +166,13 @@
                 ).start()
                 return carry
 
-            lax.fori_loop(1 if away == 0 else 0, SIDES, send, 0, unroll=7 if away == 0 else 8)
+            lax.fori_loop(1, SIDES, send, 0, unroll=7)
+
+            @pl.when(z != place_z)
+            def _(plane=plane, send=send):
+                send(0, 0)
         mine = pltpu.make_async_copy(
-            source.at[pl.ds(CAP2 * o, CAP2)], target.at[pl.ds(CAP2 * o, CAP2)], own_sem.at[index - 1]
+            block(source, o), block(target, o), own_sem.at[index - 1]
         )
         mine.start()
         return mine
@@ -175,7 +183,7 @@
     def wait_bytes(part, semaphore):
         pltpu.make_async_copy(part, part, semaphore).wait()
 
-    mine_forward = exchange(forwarded, landed, 1, FAR_FIRST)
+    mine_forward = exchange(forwarded, landed, 1, FROM_FAR)
 
     loads[4].wait()
     loads[5].wait()
@@ -208,7 +216,8 @@
     look_spaced = look[...] + 8 * lax.shift_right_logical(look[...] * 2731, 16)
     look_hot = hot(iota((MEMBERS * PAD1, LOOKS), 0) == look_spaced)
     eye = hot(iota((LOOKS, LOOKS), 0) == iota((LOOKS, LOOKS), 1))
-    from_look = lax.dot_general(eye, look_hot, (((1,), (1,)), ((), ())), preferred_element_type=F32).astype(BF16)
+    turned_look = lax.dot_general(eye, look_hot, (((1,), (1,)), ((), ())), preferred_element_type=F32)
+    from_look[...] = turned_look.astype(BF16)
 
     mine_forward.wait()
     wait_bytes(rows_of(landed, SLOTS - CAP2), recv_sem.at[1])
@@ -217,8 +226,8 @@
     slot_grads = sums[:, :WIDTH] + (sums[:, WIDTH : 2 * WIDTH] + sums[:, 2 * WIDTH :])
     slot_accum = old_accum + jnp.mean(slot_grads * slot_grads, axis=1, keepdims=True)
     fresh_slots = old_rows - learn_rate * slot_grads / jnp.sqrt(slot_accum)
-    picked[...] = fresh_slots.astype(BF16).astype(F32)
-    mine_picked = exchange(picked, returned, 2, FAR_FIRST)
+    picked[...] = fresh_slots.astype(BF16).reshape(GROUPS, CAP2, WIDTH)
+    mine_picked = exchange(picked, returned, 2, FROM_NEAR)
 
     turned = jnp.transpose(jnp.concatenate([accum[...]] * (WIDTH // 8), axis=0))
     next_accum = jnp.zeros((WIDTH, WIDTH), F32)
@@ -233,8 +242,8 @@
     new_accum[...] = jnp.transpose(next_accum)[: ROWS // WIDTH]
 
     mine_picked.wait()
-    wait_bytes(rows_of(returned, SLOTS - CAP2), recv_sem.at[2])
-    gathered = jnp.dot(from_group, returned[...].astype(BF16), preferred_element_type=F32)
+    wait_bytes(rows_of(returned, GROUPS - 1), recv_sem.at[2])
+    gathered = jnp.dot(from_group, returned[...].reshape(SLOTS, WIDTH), preferred_element_type=F32)
     back[...] = gathered.astype(BF16).reshape(MEMBERS, PAD1, WIDTH)
     for p in node_peers:
         pltpu.make_async_remote_copy(
@@ -244,22 +253,23 @@
 
     landing = reached.at[pl.ds(0, MEMBERS - 1)]
     wait_bytes(landing, recv_sem.at[3])
-    read = jnp.dot(from_look, reached[...].reshape(MEMBERS * PAD1, WIDTH), preferred_element_type=F32)
-    fresh[...] = read.astype(BF16)
 
     wait_bytes(routed.at[pl.ds(0, MEMBERS - 1)], send_sem.at[0])
     wait_bytes(rows_of(forwarded, SLOTS - CAP2), send_sem.at[1])
-    wait_bytes(rows_of(picked, SLOTS - CAP2), send_sem.at[2])
+    wait_bytes(rows_of(picked, GROUPS - 1), send_sem.at[2])
     wait_bytes(back.at[pl.ds(0, MEMBERS - 1)], send_sem.at[3])
 
 
-def hand_over(table, accum, fresh, table_out, accum_out, fresh_out, sem):
+def hand_over(table, accum, from_look, reached, table_out, accum_out, fresh_out, fresh, sem):
     copies = [
         pltpu.make_async_copy(source, target, sem.at[i])
-        for i, (source, target) in enumerate(((table, table_out), (fresh, fresh_out), (accum, accum_out)))
+        for i, (source, target) in enumerate(((table, table_out), (accum, accum_out), (fresh, fresh_out)))
     ]
-    for copy in copies:
-        copy.start()
+    copies[0].start()
+    copies[1].start()
+    read = jnp.dot(from_look[...], reached[...].reshape(MEMBERS * PAD1, WIDTH), preferred_element_type=F32)
+    fresh[...] = read.astype(BF16)
+    copies[2].start()
     for copy in copies:
         copy.wait()
 
@@ -270,10 +280,11 @@
         out_shape=(
             jax.ShapeDtypeStruct((ROWS, WIDTH), F32),
             jax.ShapeDtypeStruct((ROWS // WIDTH, WIDTH), F32),
-            jax.ShapeDtypeStruct((LOOKS, WIDTH), BF16),
+            jax.ShapeDtypeStruct((LOOKS, MEMBERS * PAD1), BF16),
+            jax.ShapeDtypeStruct((MEMBERS, PAD1, WIDTH), BF16),
         ),
         in_specs=[pl.BlockSpec(memory_space=pltpu.HBM)] * 7,
-        out_specs=[pl.BlockSpec(memory_space=pltpu.VMEM)] * 3,
+        out_specs=[pl.BlockSpec(memory_space=pltpu.VMEM)] * 4,
         scratch_shapes=[
             pltpu.VMEM((BAGS, WIDTH), F32),
             pltpu.VMEM((1, BAGS), jnp.int32),
@@ -286,9 +297,8 @@
             pltpu.VMEM((MEMBERS, CAP1, WIDTH), F32),
             pltpu.VMEM((SLOTS, WIDTH), F32),
             pltpu.VMEM((SLOTS, WIDTH), F32),
-            pltpu.VMEM((SLOTS, WIDTH), F32),
-            pltpu.VMEM((SLOTS, WIDTH), F32),
-            pltpu.VMEM((MEMBERS, PAD1, WIDTH), BF16),
+            pltpu.VMEM((GROUPS, CAP2, WIDTH), BF16),
+            pltpu.VMEM((GROUPS, CAP2, WIDTH), BF16),
             pltpu.VMEM((MEMBERS, PAD1, WIDTH), BF16),
             pltpu.SemaphoreType.DMA((7,)),
             pltpu.SemaphoreType.DMA((2,)),
@@ -303,10 +313,14 @@
     )
     table, accum, fresh = pl.pallas_call(
         hand_over,
-        out_shape=[jax.ShapeDtypeStruct(out.shape, out.dtype) for out in outs],
-        in_specs=[pl.BlockSpec(memory_space=pltpu.VMEM)] * 3,
+        out_shape=[
+            jax.ShapeDtypeStruct((ROWS, WIDTH), F32),
+            jax.ShapeDtypeStruct((ROWS // WIDTH, WIDTH), F32),
+            jax.ShapeDtypeStruct((LOOKS, WIDTH), BF16),
+        ],
+        in_specs=[pl.BlockSpec(memory_space=pltpu.VMEM)] * 4,
         out_specs=[pl.BlockSpec(memory_space=pltpu.HBM)] * 3,
-        scratch_shapes=[pltpu.SemaphoreType.DMA((3,))],
+        scratch_shapes=[pltpu.VMEM((LOOKS, WIDTH), BF16), pltpu.SemaphoreType.DMA((3,))],
         compiler_params=pltpu.CompilerParams(vmem_limit_bytes=16 * 1024 * 1024),
         cost_estimate=pl.CostEstimate(flops=0, bytes_accessed=1_400_000, transcendentals=0),
     )(*outs)

time: 46.3 us -> 44.2 us (0.955)
  Pallas kernels: 45.5 us -> 43.4 us
    pallas_call x1, Pallas kernels: 44.7 us -> 42.5 us  [on_device(): pl.pallas_call(kernel, out_shape=(jax.ShapeDtypeStruct((ROWS, WIDTH), F32...]
where the time goes in v3:
time: 44.2 us; the launch traced here: 44 us
  Pallas kernels  43.4 us (98%)
  between operations  0.64 us (1%)
    pallas_call x1, Pallas kernels, on_device(): pl.pallas_call(kernel, out_shape=(jax.ShapeDtypeStruct((ROWS, WIDTH), F32...  42.5 us
    pallas_call x1, Pallas kernels, on_device(): pl.pallas_call(hand_over, out_shape=[jax.ShapeDtypeStruct((ROWS, WIDTH),...  0.91 us

profile of v3, /device:TPU:1, one launch (start us, length us, event | category | flops | bytes accessed | tf_op | source)
XLA Modules:
  0.0 44.0 jit_solution(8692917492307620737)
XLA Ops:
  0.6 42.5 %shard_map.94 = (f32[1024,128]{1,0:T(8,128)S(1)}, f32[8,128]{1,0:T(8,128)S(1)}, bf16[512,256]{1,0:T(8,128)(2,1)S(1)}, bf16[8,32,128]{2,1,0:T(8,128)(2,1)S(1)}) custom-call(f32[32,128]{1,0:T(8,128)} %grads_in.1, s32[1,32]{1,0:T(1,128)} %lengths_in.1, s32[1,512]{1,0:T(1,128)} %look_in.1, s32[1,8,24]{2,1,0:T(8,128)} %group_in.1, s32[1,2,96]{2,1,0:T(2,128)} %bitcast.5, ...), custom_call_target="tpu_custom_call" | custom-call | flops 600000000 | bytes 1400000 | tf_op jit(solution)/shard_map/pallas_call | solution.py:278
  43.1 0.9 %shard_map.95 = (f32[1024,128]{1,0:T(8,128)}, f32[8,128]{1,0:T(8,128)}, bf16[512,128]{1,0:T(8,128)(2,1)}) custom-call(f32[1024,128]{1,0:T(8,128)S(1)} %get-tuple-element.10.table, f32[8,128]{1,0:T(8,128)S(1)} %get-tuple-element.11.accum, bf16[512,256]{1,0:T(8,128)(2,1)S(1)} %get-tuple-element.12.from_look, bf16[8,32,128]{2,1,0:T(8,128)(2,1)S(1)} %get-tuple-element.13.reached), custom_call_target="tpu_custom_call" | custom-call | bytes 1400000 | tf_op jit(solution)/shard_map/pallas_call | solution.py:314

commit v4 on v3

--- a/solution.py
+++ b/solution.py
@@ -147,9 +147,6 @@
     forwarded[...] = mix(to_group, arrived[...].reshape(SLOTS, WIDTH))
     pl.semaphore_wait(side_sem, SIDES - 1)
 
-    def block(ref, group):
-        return ref.at[pl.ds(CAP2 * group, CAP2)] if len(ref.shape) == 2 else ref.at[group]
-
     def exchange(source, target, index, order):
         for place_z in order:
             plane = place_z * SIDES
@@ -157,8 +154,8 @@
             def send(i, carry, plane=plane):
                 p = plane + lax.rem(side + i, SIDES)
                 pltpu.make_async_remote_copy(
-                    block(source, p),
-                    block(target, o),
+                    source.at[pl.ds(CAP2 * p, CAP2)],
+                    target.at[pl.ds(CAP2 * o, CAP2)],
                     send_sem.at[index],
                     recv_sem.at[index],
                     device_id={"outer": p},
@@ -172,7 +169,7 @@
             def _(plane=plane, send=send):
                 send(0, 0)
         mine = pltpu.make_async_copy(
-            block(source, o), block(target, o), own_sem.at[index - 1]
+            source.at[pl.ds(CAP2 * o, CAP2)], target.at[pl.ds(CAP2 * o, CAP2)], own_sem.at[index - 1]
         )
         mine.start()
         return mine
@@ -226,7 +223,7 @@
     slot_grads = sums[:, :WIDTH] + (sums[:, WIDTH : 2 * WIDTH] + sums[:, 2 * WIDTH :])
     slot_accum = old_accum + jnp.mean(slot_grads * slot_grads, axis=1, keepdims=True)
     fresh_slots = old_rows - learn_rate * slot_grads / jnp.sqrt(slot_accum)
-    picked[...] = fresh_slots.astype(BF16).reshape(GROUPS, CAP2, WIDTH)
+    picked[...] = fresh_slots.astype(BF16).astype(F32)
     mine_picked = exchange(picked, returned, 2, FROM_NEAR)
 
     turned = jnp.transpose(jnp.concatenate([accum[...]] * (WIDTH // 8), axis=0))
@@ -242,8 +239,8 @@
     new_accum[...] = jnp.transpose(next_accum)[: ROWS // WIDTH]
 
     mine_picked.wait()
-    wait_bytes(rows_of(returned, GROUPS - 1), recv_sem.at[2])
-    gathered = jnp.dot(from_group, returned[...].reshape(SLOTS, WIDTH), preferred_element_type=F32)
+    wait_bytes(rows_of(returned, SLOTS - CAP2), recv_sem.at[2])
+    gathered = jnp.dot(from_group, returned[...].astype(BF16), preferred_element_type=F32)
     back[...] = gathered.astype(BF16).reshape(MEMBERS, PAD1, WIDTH)
     for p in node_peers:
         pltpu.make_async_remote_copy(
@@ -256,7 +253,7 @@
 
     wait_bytes(routed.at[pl.ds(0, MEMBERS - 1)], send_sem.at[0])
     wait_bytes(rows_of(forwarded, SLOTS - CAP2), send_sem.at[1])
-    wait_bytes(rows_of(picked, GROUPS - 1), send_sem.at[2])
+    wait_bytes(rows_of(picked, SLOTS - CAP2), send_sem.at[2])
     wait_bytes(back.at[pl.ds(0, MEMBERS - 1)], send_sem.at[3])
 
 
@@ -297,8 +294,8 @@
             pltpu.VMEM((MEMBERS, CAP1, WIDTH), F32),
             pltpu.VMEM((SLOTS, WIDTH), F32),
             pltpu.VMEM((SLOTS, WIDTH), F32),
-            pltpu.VMEM((GROUPS, CAP2, WIDTH), BF16),
-            pltpu.VMEM((GROUPS, CAP2, WIDTH), BF16),
+            pltpu.VMEM((SLOTS, WIDTH), F32),
+            pltpu.VMEM((SLOTS, WIDTH), F32),
             pltpu.VMEM((MEMBERS, PAD1, WIDTH), BF16),
             pltpu.SemaphoreType.DMA((7,)),
             pltpu.SemaphoreType.DMA((2,)),

time: 44.2 us -> 44.7 us (1.011)
  Pallas kernels: 43.4 us -> 43.9 us
    pallas_call x1, Pallas kernels: 42.5 us -> 43 us  [on_device(): pl.pallas_call(kernel, out_shape=(jax.ShapeDtypeStruct((ROWS, WIDTH), F32...]
where the time goes in v4:
time: 44.7 us; the launch traced here: 44.6 us
  Pallas kernels  43.9 us (98%)
  between operations  0.64 us (1%)
    pallas_call x1, Pallas kernels, on_device(): pl.pallas_call(kernel, out_shape=(jax.ShapeDtypeStruct((ROWS, WIDTH), F32...  43 us
    pallas_call x1, Pallas kernels, on_device(): pl.pallas_call(hand_over, out_shape=[jax.ShapeDtypeStruct((ROWS, WIDTH),...  0.91 us

profile of v4, /device:TPU:1, one launch (start us, length us, event | category | flops | bytes accessed | tf_op | source)
XLA Modules:
  0.0 44.6 jit_solution(2135468999361227228)
XLA Ops:
  0.6 43.0 %shard_map.94 = (f32[1024,128]{1,0:T(8,128)S(1)}, f32[8,128]{1,0:T(8,128)S(1)}, bf16[512,256]{1,0:T(8,128)(2,1)S(1)}, bf16[8,32,128]{2,1,0:T(8,128)(2,1)S(1)}) custom-call(f32[32,128]{1,0:T(8,128)} %grads_in.1, s32[1,32]{1,0:T(1,128)} %lengths_in.1, s32[1,512]{1,0:T(1,128)} %look_in.1, s32[1,8,24]{2,1,0:T(8,128)} %group_in.1, s32[1,2,96]{2,1,0:T(2,128)} %bitcast.5, ...), custom_call_target="tpu_custom_call" | custom-call | flops 600000000 | bytes 1400000 | tf_op jit(solution)/shard_map/pallas_call | solution.py:275
  43.7 0.9 %shard_map.95 = (f32[1024,128]{1,0:T(8,128)}, f32[8,128]{1,0:T(8,128)}, bf16[512,128]{1,0:T(8,128)(2,1)}) custom-call(f32[1024,128]{1,0:T(8,128)S(1)} %get-tuple-element.10.table, f32[8,128]{1,0:T(8,128)S(1)} %get-tuple-element.11.accum, bf16[512,256]{1,0:T(8,128)(2,1)S(1)} %get-tuple-element.12.from_look, bf16[8,32,128]{2,1,0:T(8,128)(2,1)S(1)} %get-tuple-element.13.reached), custom_call_target="tpu_custom_call" | custom-call | bytes 1400000 | tf_op jit(solution)/shard_map/pallas_call | solution.py:311

commit v5 on v3

--- a/solution.py
+++ b/solution.py
@@ -166,7 +166,8 @@
                 ).start()
                 return carry
 
-            lax.fori_loop(1, SIDES, send, 0, unroll=7)
+            for i in (4, 5, 3, 6, 7, 2, 1):
+                send(i, 0)
 
             @pl.when(z != place_z)
             def _(plane=plane, send=send):
@@ -243,12 +244,28 @@
 
     mine_picked.wait()
     wait_bytes(rows_of(returned, GROUPS - 1), recv_sem.at[2])
-    gathered = jnp.dot(from_group, returned[...].reshape(SLOTS, WIDTH), preferred_element_type=F32)
-    back[...] = gathered.astype(BF16).reshape(MEMBERS, PAD1, WIDTH)
-    for p in node_peers:
+    came_back = returned[...].reshape(SLOTS, WIDTH)
+
+    def give(p):
         pltpu.make_async_remote_copy(
             back.at[p], reached.at[n], send_sem.at[3], recv_sem.at[3], device_id={"node": p}, device_id_type=MESH
         ).start()
+
+    first = jnp.dot(from_group[:PAD1], came_back, preferred_element_type=F32)
+    back[0] = first.astype(BF16)
+
+    @pl.when(n != 0)
+    def _():
+        give(0)
+
+    gathered = jnp.dot(from_group[PAD1:], came_back, preferred_element_type=F32)
+    back[1:] = gathered.astype(BF16).reshape(MEMBERS - 1, PAD1, WIDTH)
+    for p in node_peers:
+
+        @pl.when(p != 0)
+        def _(p=p):
+            give(p)
+
     reached[n] = back[n]
 
     landing = reached.at[pl.ds(0, MEMBERS - 1)]

time: 44.2 us -> 44.1 us (level)
  no operation moved by 1% of the time
where the time goes in v5:
time: 44.1 us; the launch traced here: 43.9 us
  Pallas kernels  43.3 us (98%)
  between operations  0.64 us (1%)
    pallas_call x1, Pallas kernels, on_device(): pl.pallas_call(kernel, out_shape=(jax.ShapeDtypeStruct((ROWS, WIDTH), F32...  42.4 us
    pallas_call x1, Pallas kernels, on_device(): pl.pallas_call(hand_over, out_shape=[jax.ShapeDtypeStruct((ROWS, WIDTH),...  0.91 us

profile of v5, /device:TPU:1, one launch (start us, length us, event | category | flops | bytes accessed | tf_op | source)
XLA Modules:
  0.0 43.9 jit_solution(17286907995781257640)
XLA Ops:
  0.6 42.4 %shard_map.94 = (f32[1024,128]{1,0:T(8,128)S(1)}, f32[8,128]{1,0:T(8,128)S(1)}, bf16[512,256]{1,0:T(8,128)(2,1)S(1)}, bf16[8,32,128]{2,1,0:T(8,128)(2,1)S(1)}) custom-call(f32[32,128]{1,0:T(8,128)} %grads_in.1, s32[1,32]{1,0:T(1,128)} %lengths_in.1, s32[1,512]{1,0:T(1,128)} %look_in.1, s32[1,8,24]{2,1,0:T(8,128)} %group_in.1, s32[1,2,96]{2,1,0:T(2,128)} %bitcast.5, ...), custom_call_target="tpu_custom_call" | custom-call | flops 600000000 | bytes 1400000 | tf_op jit(solution)/shard_map/pallas_call | solution.py:295
  43.0 0.9 %shard_map.95 = (f32[1024,128]{1,0:T(8,128)}, f32[8,128]{1,0:T(8,128)}, bf16[512,128]{1,0:T(8,128)(2,1)}) custom-call(f32[1024,128]{1,0:T(8,128)S(1)} %get-tuple-element.10.table, f32[8,128]{1,0:T(8,128)S(1)} %get-tuple-element.11.accum, bf16[512,256]{1,0:T(8,128)(2,1)S(1)} %get-tuple-element.12.from_look, bf16[8,32,128]{2,1,0:T(8,128)(2,1)S(1)} %get-tuple-element.13.reached), custom_call_target="tpu_custom_call" | custom-call | bytes 1400000 | tf_op jit(solution)/shard_map/pallas_call | solution.py:331
